TPU v7x, 128 devices: a whole 4x4x4 slice. The times are simulated.
128 devices in a mesh: cluster: 4 (over y_lo, core), sub: 32 (over z, y_hi, x).
Axes of the slice: x: 4, y: 4 (y_hi: 2, y_lo: 2; y = y_hi * 2 + y_lo), z: 4, core: 2. Of those that a mesh axis runs over, the one named last changes fastest.
Arguments:
- load: float32 [229376, 256], P(('cluster', 'sub'))
- schur: float32 [229376, 1792], P(('cluster', 'sub')), as said below
- modes: float32 [229376, 128], P(('cluster', 'sub')), may hold values from -0.125 to 0.125
- coarse_inverse: float32 [16384, 4096], P(('cluster', 'sub')), as said below
- interface_rows: int32 [128], P(('cluster', 'sub')), may hold values from 896 to 1792, as said below
- mode_count: int32 [128], P(('cluster', 'sub')), may hold values from 64 to 128, as said below
- left_rows: int32 [128, 384], P(('cluster', 'sub')), may hold values from 0 to 1792, as said below
- right_rows: int32 [128, 384], P(('cluster', 'sub')), may hold values from 0 to 1792, as said below
Outputs:
- solution: float32 [229376, 256], P(('cluster', 'sub'))
- residual: float32 [229376, 256], P(('cluster', 'sub'))
Inputs may be any that keep to these rules, and one draw needn't show every extreme that they name: `interface_rows`: every subdomain has at least half of 1792 live rows, and some subdomain has exactly 1792. `mode_count`: every subdomain has at least half of 128 live modes, and some subdomain has exactly 128. Slot j of right_rows[g] and slot j of left_rows[g + 1] name the same interface unknown; the used slots of a row come first, all other slots hold 1792. Two neighbours share at least half of 384 rows and some pair shares exactly 384. The used entries of left_rows[g] and right_rows[g] are distinct live rows of g. left_rows[0] and right_rows[127] are unused. `right_rows`: see left_rows. `schur`: each block S_g is symmetric positive definite with a positive diagonal. `coarse_inverse`: each cluster's coarse inverse is symmetric positive definite.
All inputs are finite; a program needn't handle non-finite values.
Results may differ from a plain program's by a relative error of at most 0.0001.
Values sent between devices are 32-bit elements; how exact they have to be, the bound alone decides.
A program may use at most 128 MiB of HBM per device.

v0:
```python
import jax
import jax.numpy as jnp
from jax import lax
from jax.sharding import PartitionSpec as P

ITERS = 3


def passed_along(value, axis, by):
    devices = lax.axis_size(axis)
    pairs = [(i, i + by) for i in range(devices) if 0 <= i + by < devices]
    return lax.ppermute(value, axis, pairs)


def take_rows(field, indices):
    return jnp.take(field, indices, axis=0, mode="fill", fill_value=0.0)


def assemble(field, left_index, right_index):
    to_left = take_rows(field, left_index)
    to_right = take_rows(field, right_index)
    from_left = passed_along(to_right, ("cluster", "sub"), 1)
    from_right = passed_along(to_left, ("cluster", "sub"), -1)
    merged = field.at[left_index].add(from_left, mode="drop")
    return merged.at[right_index].add(from_right, mode="drop")


def local(load, schur, modes, coarse_inverse, interface_rows, mode_count, left_rows, right_rows):
    highest = lax.Precision.HIGHEST
    order = schur.shape[0]
    mode_total = modes.shape[1]
    left_index = left_rows[0]
    right_index = right_rows[0]
    positions = jnp.arange(order, dtype=jnp.int32)
    live = (positions < interface_rows[0]).astype(jnp.float32)
    ones_shared = jnp.ones((left_index.shape[0],), jnp.float32)
    counted = jnp.zeros((order,), jnp.float32).at[left_index].add(ones_shared, mode="drop")
    counted = counted.at[right_index].add(ones_shared, mode="drop")
    share = (live / (1.0 + counted))[:, None]
    live_column = live[:, None]
    mode_live = (jnp.arange(mode_total, dtype=jnp.int32) < mode_count[0]).astype(jnp.float32)[
        :, None
    ]
    schur_diag = jnp.diagonal(schur)[:, None]
    rhs = assemble(live_column * load, left_index, right_index)
    solution = jnp.zeros_like(rhs)
    residual = rhs
    for iteration in range(ITERS):
        modal = jnp.einsum(
            "im,ik->mk",
            modes,
            share * residual,
            precision=highest,
            preferred_element_type=jnp.float32,
        )
        modal = modal * mode_live
        correction = jnp.dot(
            coarse_inverse,
            lax.all_gather(modal, "sub", axis=0, tiled=True),
            precision=highest,
            preferred_element_type=jnp.float32,
        )
        correction = correction * mode_live
        prolonged = jnp.dot(
            modes, correction, precision=highest, preferred_element_type=jnp.float32
        )
        direction = assemble(share * (prolonged + residual / schur_diag), left_index, right_index)
        product = jnp.dot(schur, direction, precision=highest, preferred_element_type=jnp.float32)
        image = assemble(live_column * product, left_index, right_index)
        numerator, denominator = lax.psum(
            (jnp.sum(share * residual * image, axis=0), jnp.sum(share * image * image, axis=0)),
            ("cluster", "sub"),
        )
        alpha = (numerator / (denominator + 1e-06))[None, :]
        solution = solution + alpha * direction
        residual = residual - alpha * image
    return (solution, residual)


def solution(mesh):
    return jax.shard_map(
        local,
        mesh=mesh,
        in_specs=(
            P(("cluster", "sub"), None),
            P(("cluster", "sub"), None),
            P(("cluster", "sub"), None),
            P(("cluster", "sub"), None),
            P(("cluster", "sub")),
            P(("cluster", "sub")),
            P(("cluster", "sub"), None),
            P(("cluster", "sub"), None),
        ),
        out_specs=(P(("cluster", "sub"), None), P(("cluster", "sub"), None)),
        check_vma=False,
    )
```

profile of v0, /device:TPU:1, one launch (start us, length us, event | category | flops | bytes accessed | tf_op | source)
XLA Modules:
  0.0 871.6 jit_solution(11478079976239884036)
XLA Ops:
  8.8 3.0 broadcast_multiply_fusion
  11.8 3.2 gather_fusion.1
  15.8 3.9 collective-permute-start
  19.9 3.2 gather_fusion.2
  23.9 9.8 %collective-permute-start.1 = (f32[384,256]{1,0:T(8,128)}, f32[384,256]{1,0:T(8,128)S(1)}, u32[]{:S(2)}, u32[]{:S(2)}) collective-permute-start(f32[384,256]{1,0:T(8,128)} %broadcast_select_fusion.12), channel_id=1, source_target_pairs={{1,0},{2,1},{3,2},{4,3},{5,4},{6,5},{7,6},{8,7},{9,8},{10,9},{11,1... | collective-permute-start | bytes 1179656 | tf_op jit(solution)/shard_map/ppermute | solution.py:12
  34.4 3.5 scatter_custom_fusion
  37.9 3.6 scatter_fusion
  41.6 5.1 scatter_fusion.1
  46.7 5.1 scatter_fusion.2
  54.6 3.8 fusion.15
  58.7 28.0 %gather_fusion = f32[1792]{0:T(1024)S(1)} fusion(f32[1792,1792]{1,0:T(8,128)} %param.11, s32[1792]{0:T(1024)S(1)} %or_reduce_fusion), kind=kCustom, calls=%fused_computation.14 | custom fusion | bytes 28672 | tf_op jit(solution)/shard_map/jit(diagonal)/cond/branch_0_fun/gather | solution.py:44
  86.7 49.1 %all-gather.4.cloned.1.call-done = f32[4096,256]{0,1:T(8,128)} async-done(((f32[128,256]{0,1:T(8,128)}), f32[4096,256]{0,1:T(8,128)}) %all-gather.4.cloned.1.call-update) | async-done | bytes 4194320 | tf_op jit(solution)/shard_map/all_gather | solution.py:59
  135.8 5.4 convolution_multiply_fusion.5
  141.2 2.9 add_multiply_fusion.2
  146.9 3.2 gather_fusion.4
  150.1 3.7 gather_fusion.3
  154.9 3.1 collective-permute-start.2
  158.9 8.2 collective-permute-start.3
  167.0 6.9 collective-permute-done.2
  174.0 5.6 scatter_fusion.3
  179.6 5.3 scatter_fusion.4
  184.9 27.6 %fusion = f32[1792,256]{0,1:T(8,128)} fusion(f32[1792,256]{1,0:T(8,128)} %scatter_fusion.4, f32[1792,1792]{1,0:T(8,128)} %param.11, f32[1792]{0:T(1024)S(1)} %fusion.33), kind=kOutput, calls=%fused_computation.40 | convolution fusion | flops 9865461760 | bytes 16522240 | tf_op jit(solution)/shard_map/dot_general | solution.py:68
  215.2 3.5 gather_fusion.6
  218.8 3.7 gather_fusion.5
  226.4 9.4 %collective-permute-start.5 = (f32[384,256]{1,0:T(8,128)}, f32[384,256]{1,0:T(8,128)S(1)}, u32[]{:S(2)}, u32[]{:S(2)}) collective-permute-start(f32[384,256]{1,0:T(8,128)} %broadcast_select_fusion.8), channel_id=1, source_target_pairs={{1,0},{2,1},{3,2},{4,3},{5,4},{6,5},{7,6},{8,7},{9,8},{10,9},{11,1... | collective-permute-start | bytes 1179656 | tf_op jit(solution)/shard_map/ppermute | solution.py:12
  235.7 5.9 collective-permute-done.4
  241.6 5.6 scatter_fusion.5
  247.1 5.1 scatter_fusion.6
  257.5 62.2 %all-reduce.2 = (f32[256]{0:T(256)S(1)}, f32[256]{0:T(256)S(1)}) all-reduce(f32[256]{0:T(256)S(1)} %get-tuple-element.12, f32[256]{0:T(256)S(1)} %get-tuple-element.11), channel_id=1, replica_groups=mesh['cluster'=4,'sub'=32] {'cluster','sub'}, use_global_device_ids=true, to_apply=%region_9.11 | all-reduce | flops 512 | bytes 4096 | tf_op jit(solution)/shard_map/psum | solution.py:70
  325.5 78.0 %all-gather.6.cloned.1.call-done = f32[4096,256]{0,1:T(8,128)} async-done(((f32[128,256]{0,1:T(8,128)}), f32[4096,256]{0,1:T(8,128)}) %all-gather.6.cloned.1.call-update) | async-done | bytes 4194320 | tf_op jit(solution)/shard_map/all_gather | solution.py:59
  403.5 5.5 convolution_multiply_fusion.4
  414.7 3.2 gather_fusion.8
  417.9 3.7 gather_fusion.7
  422.7 3.1 collective-permute-start.6
  426.7 8.2 collective-permute-start.7
  434.9 6.9 collective-permute-done.6
  441.8 5.6 scatter_fusion.7
  447.4 5.1 scatter_fusion.8
  452.5 27.9 %fusion.1 = f32[1792,256]{0,1:T(8,128)} fusion(f32[1792,256]{1,0:T(8,128)} %scatter_fusion.8, f32[1792,1792]{1,0:T(8,128)} %param.11, f32[1792]{0:T(1024)S(1)} %fusion.33), kind=kOutput, calls=%fused_computation.41 | convolution fusion | flops 9865461760 | bytes 16522240 | tf_op jit(solution)/shard_map/dot_general | solution.py:68
  483.2 3.3 gather_fusion.10
  486.5 3.7 gather_fusion.9
  494.1 9.4 %collective-permute-start.9 = (f32[384,256]{1,0:T(8,128)}, f32[384,256]{1,0:T(8,128)S(1)}, u32[]{:S(2)}, u32[]{:S(2)}) collective-permute-start(f32[384,256]{1,0:T(8,128)} %broadcast_select_fusion.4), channel_id=1, source_target_pairs={{1,0},{2,1},{3,2},{4,3},{5,4},{6,5},{7,6},{8,7},{9,8},{10,9},{11,1... | collective-permute-start | bytes 1179656 | tf_op jit(solution)/shard_map/ppermute | solution.py:12
  503.5 5.9 collective-permute-done.8
  509.3 5.6 scatter_fusion.9
  514.9 5.1 scatter_fusion.10
  525.3 62.1 %all-reduce.1 = (f32[256]{0:T(256)S(1)}, f32[256]{0:T(256)S(1)}) all-reduce(f32[256]{0:T(256)S(1)} %get-tuple-element.10, f32[256]{0:T(256)S(1)} %get-tuple-element.9), channel_id=1, replica_groups=mesh['cluster'=4,'sub'=32] {'cluster','sub'}, use_global_device_ids=true, to_apply=%region_17.19 | all-reduce | flops 512 | bytes 4096 | tf_op jit(solution)/shard_map/psum | solution.py:70
  593.2 78.1 %all-gather.8.cloned.1.call-done = f32[4096,256]{0,1:T(8,128)} async-done(((f32[128,256]{0,1:T(8,128)}), f32[4096,256]{0,1:T(8,128)}) %all-gather.8.cloned.1.call-update) | async-done | bytes 4194320 | tf_op jit(solution)/shard_map/all_gather | solution.py:59
  671.3 5.4 convolution_multiply_fusion.3
  676.7 2.9 add_multiply_fusion
  682.4 3.2 gather_fusion.12
  685.6 3.2 gather_fusion.11
  688.9 3.1 collective-permute-start.10
  692.1 8.2 collective-permute-start.11
  700.3 7.6 collective-permute-done.10
  707.9 5.2 scatter_fusion.11
  713.0 5.2 scatter_fusion.12
  718.2 27.9 %fusion.2 = f32[1792,256]{0,1:T(8,128)} fusion(f32[1792,256]{1,0:T(8,128)} %scatter_fusion.12, f32[1792,1792]{1,0:T(8,128)} %param.11, f32[1792]{0:T(1024)S(1)} %fusion.33), kind=kOutput, calls=%fused_computation.42 | convolution fusion | flops 9865461760 | bytes 16522240 | tf_op jit(solution)/shard_map/dot_general | solution.py:68
  749.0 3.3 gather_fusion.14
  752.3 3.2 gather_fusion.13
  758.4 9.4 %collective-permute-start.13 = (f32[384,256]{1,0:T(8,128)S(1)}, f32[384,256]{1,0:T(8,128)S(1)}, u32[]{:S(2)}, u32[]{:S(2)}) collective-permute-start(f32[384,256]{1,0:T(8,128)S(1)} %broadcast_select_fusion), channel_id=1, source_target_pairs={{1,0},{2,1},{3,2},{4,3},{5,4},{6,5},{7,6},{8,7},{9,8},{10,9},{11,1... | collective-permute-start | bytes 1179656 | tf_op jit(solution)/shard_map/ppermute | solution.py:12
  776.0 5.2 scatter_fusion.13
  781.2 5.2 scatter_fusion.14
  791.6 61.7 %all-reduce = (f32[256]{0:T(256)S(1)}, f32[256]{0:T(256)S(1)}) all-reduce(f32[256]{0:T(256)S(1)} %get-tuple-element.8, f32[256]{0:T(256)S(1)} %get-tuple-element.7), channel_id=1, replica_groups=mesh['cluster'=4,'sub'=32] {'cluster','sub'}, use_global_device_ids=true, to_apply=%region_25.27 | all-reduce | flops 512 | bytes 4096 | tf_op jit(solution)/shard_map/psum | solution.py:70
  853.3 6.1 multiply_subtract_fusion
  (91 shorter events, 81.3 us)
Async XLA Ops:
  7.2 128.6 %copy-start = (f32[128,4096]{1,0:T(8,128)S(1)}, f32[128,4096]{1,0:T(8,128)}, u32[]{:S(2)}) copy-start(f32[128,4096]{1,0:T(8,128)} %param.13) | copy-start | bytes 6291460
  7.2 128.6 %all-gather.4.cloned.1.call-start = ((), (), s32[]{:S(2)}) async-start(), calls=%async_computation | async-start | bytes 4325376 | tf_op jit(solution)/shard_map/all_gather | solution.py:59
  11.8 8.0 copy-start.7
  15.8 25.8 %collective-permute-start = (f32[384,256]{1,0:T(8,128)}, f32[384,256]{1,0:T(8,128)S(1)}, u32[]{:S(2)}, u32[]{:S(2)}) collective-permute-start(f32[384,256]{1,0:T(8,128)} %broadcast_select_fusion.13), channel_id=1, source_target_pairs={{0,1},{1,2},{2,3},{3,4},{4,5},{5,6},{6,7},{7,8},{8,9},{9,10},{10,1... | collective-permute-start | bytes 1179656 | tf_op jit(solution)/shard_map/ppermute | solution.py:12
  19.9 18.1 %copy-start.8 = (s32[1,384]{1,0:T(1,128)S(1)}, s32[1,384]{1,0:T(1,128)}, u32[]{:S(2)}) copy-start(s32[1,384]{1,0:T(1,128)} %param.17) | copy-start | bytes 4612
  23.9 22.8 %collective-permute-start.1 = (f32[384,256]{1,0:T(8,128)}, f32[384,256]{1,0:T(8,128)S(1)}, u32[]{:S(2)}, u32[]{:S(2)}) collective-permute-start(f32[384,256]{1,0:T(8,128)} %broadcast_select_fusion.12), channel_id=1, source_target_pairs={{1,0},{2,1},{3,2},{4,3},{5,4},{6,5},{7,6},{8,7},{9,8},{10,9},{11,1... | collective-permute-start | bytes 1179656 | tf_op jit(solution)/shard_map/ppermute | solution.py:12
  51.8 2.8 copy-start.6
  58.4 345.1 %all-gather.6.cloned.1.call-start = ((), (), s32[]{:S(2)}) async-start(), calls=%async_computation.1 | async-start | bytes 4325376 | tf_op jit(solution)/shard_map/all_gather | solution.py:59
  135.8 5.4 copy-start.1
  154.9 19.1 %collective-permute-start.2 = (f32[384,256]{1,0:T(8,128)S(1)}, f32[384,256]{1,0:T(8,128)}, u32[]{:S(2)}, u32[]{:S(2)}) collective-permute-start(f32[384,256]{1,0:T(8,128)S(1)} %broadcast_select_fusion.11), channel_id=1, source_target_pairs={{0,1},{1,2},{2,3},{3,4},{4,5},{5,6},{6,7},{7,8},{8,9},{9,10},{10,1... | collective-permute-start | bytes 1179656 | tf_op jit(solution)/shard_map/ppermute | solution.py:12
  158.9 20.7 %collective-permute-start.3 = (f32[384,256]{1,0:T(8,128)}, f32[384,256]{1,0:T(8,128)S(1)}, u32[]{:S(2)}, u32[]{:S(2)}) collective-permute-start(f32[384,256]{1,0:T(8,128)} %broadcast_select_fusion.10), channel_id=1, source_target_pairs={{1,0},{2,1},{3,2},{4,3},{5,4},{6,5},{7,6},{8,7},{9,8},{10,9},{11,1... | collective-permute-start | bytes 1179656 | tf_op jit(solution)/shard_map/ppermute | solution.py:12
  223.6 18.0 %collective-permute-start.4 = (f32[384,256]{1,0:T(8,128)S(1)}, f32[384,256]{1,0:T(8,128)}, u32[]{:S(2)}, u32[]{:S(2)}) collective-permute-start(f32[384,256]{1,0:T(8,128)S(1)} %broadcast_select_fusion.9), channel_id=1, source_target_pairs={{0,1},{1,2},{2,3},{3,4},{4,5},{5,6},{6,7},{7,8},{8,9},{9,10},{10,1... | collective-permute-start | bytes 1179656 | tf_op jit(solution)/shard_map/ppermute | solution.py:12
  226.4 20.8 %collective-permute-start.5 = (f32[384,256]{1,0:T(8,128)}, f32[384,256]{1,0:T(8,128)S(1)}, u32[]{:S(2)}, u32[]{:S(2)}) collective-permute-start(f32[384,256]{1,0:T(8,128)} %broadcast_select_fusion.8), channel_id=1, source_target_pairs={{1,0},{2,1},{3,2},{4,3},{5,4},{6,5},{7,6},{8,7},{9,8},{10,9},{11,1... | collective-permute-start | bytes 1179656 | tf_op jit(solution)/shard_map/ppermute | solution.py:12
  321.9 1.2 copy-start.2
  325.5 345.8 %all-gather.8.cloned.1.call-start = ((), (), s32[]{:S(2)}) async-start(), calls=%async_computation.2 | async-start | bytes 4325376 | tf_op jit(solution)/shard_map/all_gather | solution.py:59
  403.5 5.5 copy-start.3
  422.7 19.1 %collective-permute-start.6 = (f32[384,256]{1,0:T(8,128)S(1)}, f32[384,256]{1,0:T(8,128)}, u32[]{:S(2)}, u32[]{:S(2)}) collective-permute-start(f32[384,256]{1,0:T(8,128)S(1)} %broadcast_select_fusion.7), channel_id=1, source_target_pairs={{0,1},{1,2},{2,3},{3,4},{4,5},{5,6},{6,7},{7,8},{8,9},{9,10},{10,1... | collective-permute-start | bytes 1179656 | tf_op jit(solution)/shard_map/ppermute | solution.py:12
  426.7 20.7 %collective-permute-start.7 = (f32[384,256]{1,0:T(8,128)}, f32[384,256]{1,0:T(8,128)S(1)}, u32[]{:S(2)}, u32[]{:S(2)}) collective-permute-start(f32[384,256]{1,0:T(8,128)} %broadcast_select_fusion.6), channel_id=1, source_target_pairs={{1,0},{2,1},{3,2},{4,3},{5,4},{6,5},{7,6},{8,7},{9,8},{10,9},{11,1... | collective-permute-start | bytes 1179656 | tf_op jit(solution)/shard_map/ppermute | solution.py:12
  491.3 18.0 %collective-permute-start.8 = (f32[384,256]{1,0:T(8,128)S(1)}, f32[384,256]{1,0:T(8,128)}, u32[]{:S(2)}, u32[]{:S(2)}) collective-permute-start(f32[384,256]{1,0:T(8,128)S(1)} %broadcast_select_fusion.5), channel_id=1, source_target_pairs={{0,1},{1,2},{2,3},{3,4},{4,5},{5,6},{6,7},{7,8},{8,9},{9,10},{10,1... | collective-permute-start | bytes 1179656 | tf_op jit(solution)/shard_map/ppermute | solution.py:12
  494.1 20.8 %collective-permute-start.9 = (f32[384,256]{1,0:T(8,128)}, f32[384,256]{1,0:T(8,128)S(1)}, u32[]{:S(2)}, u32[]{:S(2)}) collective-permute-start(f32[384,256]{1,0:T(8,128)} %broadcast_select_fusion.4), channel_id=1, source_target_pairs={{1,0},{2,1},{3,2},{4,3},{5,4},{6,5},{7,6},{8,7},{9,8},{10,9},{11,1... | collective-permute-start | bytes 1179656 | tf_op jit(solution)/shard_map/ppermute | solution.py:12
  589.7 1.2 copy-start.4
  671.3 5.4 copy-start.5
  688.9 19.0 %collective-permute-start.10 = (f32[384,256]{1,0:T(8,128)S(1)}, f32[384,256]{1,0:T(8,128)S(1)}, u32[]{:S(2)}, u32[]{:S(2)}) collective-permute-start(f32[384,256]{1,0:T(8,128)S(1)} %broadcast_select_fusion.3), channel_id=1, source_target_pairs={{0,1},{1,2},{2,3},{3,4},{4,5},{5,6},{6,7},{7,8},{8,9},{9,10},{10,1... | collective-permute-start | bytes 1179656 | tf_op jit(solution)/shard_map/ppermute | solution.py:12
  692.1 20.9 %collective-permute-start.11 = (f32[384,256]{1,0:T(8,128)S(1)}, f32[384,256]{1,0:T(8,128)S(1)}, u32[]{:S(2)}, u32[]{:S(2)}) collective-permute-start(f32[384,256]{1,0:T(8,128)S(1)} %broadcast_select_fusion.2), channel_id=1, source_target_pairs={{1,0},{2,1},{3,2},{4,3},{5,4},{6,5},{7,6},{8,7},{9,8},{10,9},{11,1... | collective-permute-start | bytes 1179656 | tf_op jit(solution)/shard_map/ppermute | solution.py:12
  756.3 19.7 %collective-permute-start.12 = (f32[384,256]{1,0:T(8,128)}, f32[384,256]{1,0:T(8,128)S(1)}, u32[]{:S(2)}, u32[]{:S(2)}) collective-permute-start(f32[384,256]{1,0:T(8,128)} %broadcast_select_fusion.1), channel_id=1, source_target_pairs={{0,1},{1,2},{2,3},{3,4},{4,5},{5,6},{6,7},{7,8},{8,9},{9,10},{10,1... | collective-permute-start | bytes 1179656 | tf_op jit(solution)/shard_map/ppermute | solution.py:12
  758.4 22.8 %collective-permute-start.13 = (f32[384,256]{1,0:T(8,128)S(1)}, f32[384,256]{1,0:T(8,128)S(1)}, u32[]{:S(2)}, u32[]{:S(2)}) collective-permute-start(f32[384,256]{1,0:T(8,128)S(1)} %broadcast_select_fusion), channel_id=1, source_target_pairs={{1,0},{2,1},{3,2},{4,3},{5,4},{6,5},{7,6},{8,7},{9,8},{10,9},{11,1... | collective-permute-start | bytes 1179656 | tf_op jit(solution)/shard_map/ppermute | solution.py:12
Sparse Core Ops, SparseCore 0:
  58.6 77.1 all-gather.3
  325.6 77.8 all-gather.5
  593.3 77.9 all-gather.7
where the time goes:
time: 882 us; the launch traced here: 872 us
  waiting for transfers between devices  238 us (27%)
  blocking collectives  186 us (21%)
  local copies, waits for them, and re-layouts  119 us (13%)
  matrix products  117 us (13%)
  other arithmetic  114 us (13%)
  starting transfers between devices  81.6 us (9%)
  between operations  15.7 us (2%)
    all_gather x3, waiting for transfers between devices, local(): lax.all_gather(modal, 'sub', axis=0, tiled=True)  205 us
    psum x3, blocking collectives, local(): lax.psum((jnp.sum(share * residual * image, axis=0), jnp.sum(share * imag...  186 us
    dot_general x3, matrix products, local(): jnp.dot(schur, direction, precision=highest, preferred_element_type=jnp.f...  83.5 us
    ppermute x14, starting transfers between devices, passed_along(): return lax.ppermute(value, axis, pairs)  81.4 us
    gather x14, local copies, waits for them, and re-layouts, take_rows(): return jnp.take(field, indices, axis=0, mode='fill', fill_value=0.0)  47.1 us
    scatter-add x7, other arithmetic, assemble(): merged = field.at[left_index].add(from_left, mode='drop')  37.7 us
    scatter-add x7, other arithmetic, assemble(): return merged.at[right_index].add(from_right, mode='drop')  36.1 us
    ppermute x14, waiting for transfers between devices, passed_along(): return lax.ppermute(value, axis, pairs)  33.2 us
  transfers between devices with their start and end apart: 17, of which 8 were waited for; matrix products, arithmetic and copies ran while one was open for 10% of the time, Pallas kernels for 0%

commit v1 on v0

v1 whole, which is shorter than its diff:
```python
import functools

import jax
import jax.numpy as jnp
from jax import lax
from jax.experimental import pallas as pl
from jax.experimental.pallas import tpu as pltpu
from jax.sharding import PartitionSpec as P

MESH = pl.DeviceIdType.MESH
F32 = jnp.float32
BF16 = jnp.bfloat16
NI = 1792
NS = 384
K = 256
NM = 128
ITERS = 3
W = 128
STREAMS = K // W
TILE = 256
ROW_TILES = NI // TILE
CHUNK = 128
CHUNKS = NI // CHUNK

ZY = [(2, 1), (2, 0), (1, 1), (3, 1), (1, 0), (3, 0), (0, 1), (0, 0)]
YC = [(dy, dc) for dy in (2, 1, 3, 0) for dc in (1, 0) if (dy, dc) != (0, 0)]
THREE = (2, 1, 3)


def split(value):
    high = value.astype(BF16)
    low = (value - high.astype(F32)).astype(BF16)
    return jnp.concatenate([high, low], axis=1)


def halves(value):
    width = value.shape[1] // 2
    return value[:, :width] + value[:, width:]


def dot(a, b):
    return jnp.dot(a, b, preferred_element_type=F32)


def each_tile(count, size, body):
    def step(i, carry):
        body(pl.ds(pl.multiple_of(i * size, size), size), i * size)
        return carry

    lax.fori_loop(0, count, step, 0)


def kernel(
    load, schur, modes, coarse, live_rows, mode_count, index_row, index_column,
    x_out, r_out,
    s_hi, s_lo, ss_hi, ss_lo, chunk, to_slots, from_slots, phi, phit_hi, phit_lo, phi3_hi, phi3_lo,
    c_in, c_hi, c_lo, share, delta, pair_send, pair_recv,
    w_buf, d_buf, two, e_send, e_recv, ag, ag_two, rs_send, rs_recv, corr, corr_w, corr_two, ar_send, ar_recv,
    local_sem, chunk_sem, send_sem, recv_sem,
):
    c = lax.axis_index("cluster")
    s = lax.axis_index("sub")
    z, yh, xx = s // 8, (s // 4) % 2, s % 4
    g = c * 32 + s

    def ring(by):
        t = (g + by + 128) % 128
        return (t // 32, t % 32)

    def x_peer(dx):
        return (c, z * 8 + yh * 4 + (xx + dx) % 4)

    def zy_line(dz, dy):
        return ((z + dz) % 4) * 2 + (yh + dy) % 2

    def zy_peer(dz, dy):
        return (c, zy_line(dz, dy) * 4 + xx)

    def yc_peer(dy, dc):
        y = (yh * 2 + c // 2 + dy) % 4
        return ((y % 2) * 2 + (c + dc) % 2, z * 8 + (y // 2) * 4 + xx)

    def back(dz, dy):
        return ZY.index(((4 - dz) % 4, (2 - dy) % 2))

    counter = [0]
    started = []

    def send(src, dst, peer):
        n = counter[0]
        counter[0] = n + 1
        copy = pltpu.make_async_remote_copy(
            src_ref=src, dst_ref=dst, send_sem=send_sem.at[n], recv_sem=recv_sem.at[n],
            device_id=peer, device_id_type=MESH,
        )
        copy.start()
        return copy

    loads = [
        pltpu.make_async_copy(load.at[:, pl.ds(h * W, W)], w_buf.at[h], local_sem.at[h])
        for h in range(STREAMS)
    ]
    loads.append(pltpu.make_async_copy(modes, phi, local_sem.at[STREAMS]))
    line = z * 2 + yh
    loads.append(
        pltpu.make_async_copy(
            coarse.at[:, pl.ds(pl.multiple_of(line * 512, 512), 512)], c_in.at[7], local_sem.at[STREAMS + 1]
        )
    )
    for copy in loads:
        copy.start()

    def chunk_copy(i):
        slot = lax.rem(i, 2)
        return pltpu.make_async_copy(
            schur.at[pl.ds(pl.multiple_of(i * CHUNK, CHUNK), CHUNK)], chunk.at[slot], chunk_sem.at[slot]
        )

    chunk_copy(0).start()
    chunk_copy(1).start()

    peers = [ring(1), ring(-1)]
    peers += [x_peer(d) for d in THREE]
    peers += [zy_peer(*d) for d in ZY[:-1]]
    peers += [yc_peer(*d) for d in YC]
    barrier = pltpu.get_barrier_semaphore()
    for peer in peers:
        pl.semaphore_signal(barrier, inc=1, device_id=peer, device_id_type=MESH)

    live_count = live_rows[0]
    modes_live = mode_count[0]

    def build_slots(rows, base):
        local = lax.broadcasted_iota(jnp.int32, (TILE, NI), 1)
        from_slots[rows] = (local == index_column[rows]).astype(F32).astype(BF16)

    each_tile(2 * NS // TILE, TILE, build_slots)

    def live_mask(base, shape):
        return (lax.broadcasted_iota(jnp.int32, shape, 0) + base) < live_count

    for h in range(STREAMS):
        loads[h].wait()

        def mask_load(rows, base, h=h):
            value = jnp.where(live_mask(base, (TILE, W)), w_buf[h, rows], 0.0)
            w_buf[h, rows] = value
            two[h, rows] = split(value)

        each_tile(ROW_TILES, TILE, mask_load)

    pl.semaphore_wait(barrier, len(peers))

    c_copies = [
        send(
            coarse.at[:, pl.ds(pl.multiple_of(zy_line(dz, dy) * 512, 512), 512)],
            c_in.at[back(dz, dy)],
            zy_peer(dz, dy),
        )
        for dz, dy in ZY[:-1]
    ]

    def exchange(src, dst):
        return [
            send(src.at[pl.ds(NS, NS)], dst.at[pl.ds(0, NS)], ring(1)),
            send(src.at[pl.ds(0, NS)], dst.at[pl.ds(NS, NS)], ring(-1)),
        ]

    def arrived(copies):
        for copy in copies:
            copy.wait_recv()

    def left(copies):
        for copy in copies:
            copy.wait_send()

    def zeros8():
        return jnp.zeros((8, W), F32)

    def fold8(value):
        return jnp.sum(value.reshape(TILE // 8, 8, W), axis=0)

    def stream(h):
        e_copies = []

        def send_shared(t):
            e_copies.append(exchange(e_send.at[h], e_recv.at[h, t]))

        def gather_load(rows, base):
            e_send[h, rows] = halves(dot(from_slots[rows], two[h]))

        each_tile(2 * NS // TILE, TILE, gather_load)
        send_shared(0)
        yield

        def receive_shared(t):
            arrived(e_copies[t])

            def cut(rows, base):
                e_two_rows = split(e_recv[h, t, rows])
                e_two[rows] = e_two_rows

            each_tile(2 * NS // TILE, TILE, cut)

        e_two = two.at[STREAMS]

        def scattered(rows):
            return halves(dot(to_slots[rows], e_two[pl.ds(0, 2 * NS)]))

        def modal_and_gather(t):
            modal = halves(dot(phit_hi[...], two[h]) + dot(phit_lo[...], two[h]))
            ag[h, t, xx] = modal
            return [send(ag.at[h, t, xx], ag.at[h, t, xx], x_peer(d)) for d in THREE]

        receive_shared(0)

        def first_residual(rows, base):
            value = w_buf[h, rows] + scattered(rows)
            r_out[rows, pl.ds(h * W, W)] = value
            two[h, rows] = split(value)

        each_tile(ROW_TILES, TILE, first_residual)
        ag_copies = modal_and_gather(0)
        yield

        def reduce_x(t):
            return [send(ar_send.at[h, t, 0], ar_recv.at[h, t, i], x_peer(d)) for i, d in enumerate(THREE)]

        def reduce_z(t, copies):
            arrived(copies)
            ar_send[h, t, 1] = ar_send[h, t, 0] + ar_recv[h, t, 0] + ar_recv[h, t, 1] + ar_recv[h, t, 2]
            return [send(ar_send.at[h, t, 1], ar_recv.at[h, t, 3 + i], zy_peer(d, 0)) for i, d in enumerate(THREE)]

        def reduce_y(t, copies):
            arrived(copies)
            ar_send[h, t, 2] = ar_send[h, t, 1] + ar_recv[h, t, 3] + ar_recv[h, t, 4] + ar_recv[h, t, 5]
            return [send(ar_send.at[h, t, 2], ar_recv.at[h, t, 6 + i], yc_peer(*d)) for i, d in enumerate(YC)]

        def reduced(t, copies):
            arrived(copies)
            total = ar_send[h, t, 2]
            for i in range(7):
                total = total + ar_recv[h, t, 6 + i]
            numerator = jnp.sum(total[:8], axis=0, keepdims=True)
            denominator = jnp.sum(total[8:], axis=0, keepdims=True)
            return numerator / (denominator + 1e-06)

        rs_copies = []
        ar_x = ar_z = ar_y = None
        everything = []
        for t in range(ITERS):
            arrived(ag_copies)
            everything += ag_copies
            for i in range(4):
                ag_two[h, pl.ds(i * NM, NM)] = split(ag[h, t, i])
            left(rs_copies)
            rs_copies = []
            for pair in range(4):
                rows = pl.ds(pair * 256, 256)
                rs_send[h, rows] = halves(dot(c_hi[rows], ag_two[h]) + dot(c_lo[rows], ag_two[h]))
                for k in (2 * pair, 2 * pair + 1):
                    if k < 7:
                        rs_copies.append(
                            send(rs_send.at[h, pl.ds(k * NM, NM)], rs_recv.at[h, t, back(*ZY[k])], zy_peer(*ZY[k]))
                        )
            if t > 0:
                ar_z = reduce_z(t - 1, ar_x)
                everything += ar_x
            yield
            arrived(rs_copies)
            total = rs_send[h, pl.ds(7 * NM, NM)]
            for k in range(7):
                total = total + rs_recv[h, t, k]
            corr_w[h, t, 0] = total
            corr_copies = [
                send(corr_w.at[h, t, 0], corr_w.at[h, t, 1], ring(1)),
                send(corr_w.at[h, t, 0], corr_w.at[h, t, 2], ring(-1)),
            ]
            if t > 0:
                ar_y = reduce_y(t - 1, ar_z)
                everything += ar_z
            yield
            if t > 0:
                alpha = reduced(t - 1, ar_y)
                everything += ar_y
            arrived(corr_copies)
            everything += corr_copies
            for i in range(3):
                value = corr_w[h, t, i]
                if t > 0:
                    value = corr[h, i] - alpha * value
                corr[h, i] = value
                corr_two[h, pl.ds(i * NM, NM)] = split(value)

            def make_direction(rows, base):
                columns = pl.ds(h * W, W)
                coarse_part = halves(dot(phi3_hi[rows], corr_two[h]) + dot(phi3_lo[rows], corr_two[h]))
                residual = r_out[rows, columns]
                if t > 0:
                    residual = residual - alpha * w_buf[h, rows]
                    r_out[rows, columns] = residual
                    step = alpha * d_buf[h, rows]
                    x_out[rows, columns] = step if t == 1 else x_out[rows, columns] + step
                value = delta[rows] * residual + coarse_part
                d_buf[h, rows] = value
                two[h, rows] = split(value)

            each_tile(ROW_TILES, TILE, make_direction)
            left(e_copies[t])

            def shared_product(rows, base):
                e_send[h, rows] = halves(dot(ss_hi[rows], two[h]) + dot(ss_lo[rows], two[h]))

            each_tile(2 * NS // TILE, TILE, shared_product)
            send_shared(t + 1)
            yield

            def product(rows, base):
                value = halves(dot(s_hi[rows], two[h]) + dot(s_lo[rows], two[h]))
                w_buf[h, rows] = jnp.where(live_mask(base, (TILE, W)), value, 0.0)

            each_tile(ROW_TILES, TILE, product)
            yield
            receive_shared(t + 1)

            def make_image(i, sums):
                base = i * TILE
                rows = pl.ds(pl.multiple_of(base, TILE), TILE)
                value = w_buf[h, rows] + scattered(rows)
                w_buf[h, rows] = value
                if t < ITERS - 1:
                    two[h, rows] = split(value)
                weighted = share[rows] * value
                return (
                    sums[0] + fold8(weighted * r_out[rows, pl.ds(h * W, W)]),
                    sums[1] + fold8(weighted * value),
                )

            numerator, denominator = lax.fori_loop(0, ROW_TILES, make_image, (zeros8(), zeros8()))
            ar_send[h, t, 0, pl.ds(0, 8)] = numerator
            ar_send[h, t, 0, pl.ds(8, 8)] = denominator
            ar_x = reduce_x(t)
            if t < ITERS - 1:
                ag_copies = modal_and_gather(t + 1)
            yield
        ar_z = reduce_z(ITERS - 1, ar_x)
        yield
        ar_y = reduce_y(ITERS - 1, ar_z)
        yield
        alpha = reduced(ITERS - 1, ar_y)

        def finish(rows, base):
            columns = pl.ds(h * W, W)
            r_out[rows, columns] = r_out[rows, columns] - alpha * w_buf[h, rows]
            x_out[rows, columns] = x_out[rows, columns] + alpha * d_buf[h, rows]

        each_tile(ROW_TILES, TILE, finish)
        left(everything + ar_x + ar_z + ar_y + rs_copies + e_copies[ITERS])
        yield

    streams = [stream(h) for h in range(STREAMS)]
    for one in streams:
        next(one)

    def build_rows(rows, base):
        local = lax.broadcasted_iota(jnp.int32, (TILE, 2 * NS), 0) + base
        hot = (local == index_row[...]).astype(F32)
        to_slots[rows] = hot.astype(BF16)
        counted = jnp.sum(hot, axis=1, keepdims=True)
        alive = jnp.where(live_mask(base, (TILE, 1)), 1.0, 0.0)
        share[rows] = jnp.broadcast_to(alive / (1.0 + counted), (TILE, W))

    each_tile(ROW_TILES, TILE, build_rows)

    def cut_chunk(i, carry):
        chunk_copy(i).wait()
        slot = lax.rem(i, 2)
        base = pl.multiple_of(i * CHUNK, CHUNK)
        rows = pl.ds(base, CHUNK)
        for part in range(7):
            columns = pl.ds(part * 256, 256)
            value = chunk[slot, :, columns]
            high = value.astype(BF16)
            s_hi[rows, columns] = high
            s_lo[rows, columns] = (value - high.astype(F32)).astype(BF16)
        block = chunk[slot, :, pl.ds(base, CHUNK)]
        same = lax.broadcasted_iota(jnp.int32, (CHUNK, CHUNK), 0) == lax.broadcasted_iota(
            jnp.int32, (CHUNK, CHUNK), 1
        )
        diagonal = jnp.sum(jnp.where(same, block, 0.0), axis=1, keepdims=True)
        delta[rows] = share[rows] / diagonal
        return carry

    def cut_and_next(i, carry):
        cut_chunk(i, carry)
        chunk_copy(i + 2).start()
        return carry

    lax.fori_loop(0, CHUNKS - 2, cut_and_next, 0)
    lax.fori_loop(CHUNKS - 2, CHUNKS, cut_chunk, 0)

    loads[STREAMS].wait()
    mode_mask = lax.broadcasted_iota(jnp.int32, (TILE, NM), 1) < modes_live

    def weigh_modes(rows, base):
        value = jnp.where(mode_mask, share[rows] * phi[rows], 0.0)
        both = split(value)
        phi3_hi[rows, pl.ds(0, NM)] = both[:, :NM]
        phi3_lo[rows, pl.ds(0, NM)] = both[:, NM:]
        phit_hi[:, rows] = value.T.astype(BF16)
        phit_lo[:, rows] = both[:, NM:].astype(F32).T.astype(BF16)
        two[STREAMS, rows] = split(delta[rows])

    each_tile(ROW_TILES, TILE, weigh_modes)

    def gather_pair(rows, base):
        hot = from_slots[rows]
        pair_send[rows, pl.ds(0, NM)] = dot(hot, phi3_hi[:, pl.ds(0, NM)]) + dot(hot, phi3_lo[:, pl.ds(0, NM)])
        pair_send[rows, pl.ds(NM, NM)] = halves(dot(hot, two[STREAMS]))

    each_tile(2 * NS // TILE, TILE, gather_pair)
    pair_copies = exchange(pair_send, pair_recv)

    for one in streams:
        next(one)

    def gather_schur(rows, base):
        hot = from_slots[rows]
        for part in range(7):
            columns = pl.ds(part * 256, 256)
            ss_hi[rows, columns] = dot(hot, s_hi[:, columns]).astype(BF16)
            ss_lo[rows, columns] = dot(hot, s_lo[:, columns]).astype(BF16)

    each_tile(2 * NS // TILE, TILE, gather_schur)

    loads[STREAMS + 1].wait()
    arrived(c_copies)
    for k in range(8):
        both = split(c_in[k])
        c_hi[pl.ds(k * NM, NM)] = both[:, :512]
        c_lo[pl.ds(k * NM, NM)] = both[:, 512:]

    for one in streams:
        next(one)

    arrived(pair_copies)

    def cut_pair(rows, base):
        value = pair_recv[rows]
        high = value.astype(BF16)
        two[STREAMS, rows] = high
        pair_send_low[rows] = (value - high.astype(F32)).astype(BF16)

    pair_send_low = two.at[STREAMS + 1]
    each_tile(2 * NS // TILE, TILE, cut_pair)

    def place_pair(rows, base):
        for side in range(2):
            slots = pl.ds(side * NS, NS)
            hot = to_slots[rows, slots]
            high = dot(hot, two[STREAMS, slots])
            low = dot(hot, pair_send_low[slots])
            columns = pl.ds((1 + side) * NM, NM)
            phi3_hi[rows, columns] = high[:, :NM].astype(BF16)
            phi3_lo[rows, columns] = low[:, :NM].astype(BF16)
            delta[rows] = delta[rows] + (high[:, NM:] + low[:, NM:])

    each_tile(ROW_TILES, TILE, place_pair)

    running = True
    while running:
        for one in streams:
            if next(one, None) is None and one.gi_frame is None:
                running = False
    left(c_copies)
    left(pair_copies)


def local(load, schur, modes, coarse_inverse, interface_rows, mode_count, left_rows, right_rows):
    index_row = jnp.concatenate([left_rows, right_rows], axis=1)
    index_column = index_row.reshape(2 * NS, 1)
    vmem = pl.BlockSpec(memory_space=pltpu.VMEM)
    smem = pl.BlockSpec(memory_space=pltpu.SMEM)
    anywhere = pl.BlockSpec(memory_space=pl.ANY)
    copies = 7 + 2 + STREAMS * (2 * (ITERS + 1) + ITERS * (3 + 7 + 2 + 3 + 3 + 7))
    return pl.pallas_call(
        kernel,
        out_shape=(jax.ShapeDtypeStruct((NI, K), F32), jax.ShapeDtypeStruct((NI, K), F32)),
        in_specs=[anywhere, anywhere, anywhere, anywhere, smem, smem, vmem, vmem],
        out_specs=(vmem, vmem),
        scratch_shapes=[
            pltpu.VMEM((NI, NI), BF16),
            pltpu.VMEM((NI, NI), BF16),
            pltpu.VMEM((2 * NS, NI), BF16),
            pltpu.VMEM((2 * NS, NI), BF16),
            pltpu.VMEM((2, CHUNK, NI), F32),
            pltpu.VMEM((NI, 2 * NS), BF16),
            pltpu.VMEM((2 * NS, NI), BF16),
            pltpu.VMEM((NI, NM), F32),
            pltpu.VMEM((NM, NI), BF16),
            pltpu.VMEM((NM, NI), BF16),
            pltpu.VMEM((NI, 3 * NM), BF16),
            pltpu.VMEM((NI, 3 * NM), BF16),
            pltpu.VMEM((8, NM, 512), F32),
            pltpu.VMEM((8 * NM, 512), BF16),
            pltpu.VMEM((8 * NM, 512), BF16),
            pltpu.VMEM((NI, W), F32),
            pltpu.VMEM((NI, W), F32),
            pltpu.VMEM((2 * NS, 2 * NM), F32),
            pltpu.VMEM((2 * NS, 2 * NM), F32),
            pltpu.VMEM((STREAMS, NI, W), F32),
            pltpu.VMEM((STREAMS, NI, W), F32),
            pltpu.VMEM((STREAMS + 2, NI, 2 * W), BF16),
            pltpu.VMEM((STREAMS, 2 * NS, W), F32),
            pltpu.VMEM((STREAMS, ITERS + 1, 2 * NS, W), F32),
            pltpu.VMEM((STREAMS, ITERS, 4, NM, W), F32),
            pltpu.VMEM((STREAMS, 4 * NM, 2 * W), BF16),
            pltpu.VMEM((STREAMS, 8 * NM, W), F32),
            pltpu.VMEM((STREAMS, ITERS, 7, NM, W), F32),
            pltpu.VMEM((STREAMS, 3, NM, W), F32),
            pltpu.VMEM((STREAMS, ITERS, 3, NM, W), F32),
            pltpu.VMEM((STREAMS, 3 * NM, 2 * W), BF16),
            pltpu.VMEM((STREAMS, ITERS, 3, 16, W), F32),
            pltpu.VMEM((STREAMS, ITERS, 13, 16, W), F32),
            pltpu.SemaphoreType.DMA((STREAMS + 2,)),
            pltpu.SemaphoreType.DMA((2,)),
            pltpu.SemaphoreType.DMA((copies,)),
            pltpu.SemaphoreType.DMA((copies,)),
        ],
        compiler_params=pltpu.CompilerParams(
            collective_id=0, has_side_effects=True, vmem_limit_bytes=62 * 1024 * 1024
        ),
        cost_estimate=pl.CostEstimate(flops=20 * 10**9, bytes_accessed=21 * 10**6, transcendentals=0),
    )(load, schur, modes, coarse_inverse, interface_rows, mode_count, index_row, index_column)


def solution(mesh):
    return jax.shard_map(
        local,
        mesh=mesh,
        in_specs=(
            P(("cluster", "sub"), None),
            P(("cluster", "sub"), None),
            P(("cluster", "sub"), None),
            P(("cluster", "sub"), None),
            P(("cluster", "sub")),
            P(("cluster", "sub")),
            P(("cluster", "sub"), None),
            P(("cluster", "sub"), None),
        ),
        out_specs=(P(("cluster", "sub"), None), P(("cluster", "sub"), None)),
        check_vma=False,
    )
```

time: 882 us -> 209 us (0.24); the launches traced: 872 us -> 209 us
  waiting for transfers between devices: 238 us -> 0 us
  Pallas kernels: 0 us -> 201 us
  blocking collectives: 186 us -> 0 us
  matrix products: 117 us -> 0 us
  other arithmetic: 114 us -> 0 us
  local copies, waits for them, and re-layouts: 119 us -> 6.52 us
  starting transfers between devices: 81.6 us -> 0 us
  between operations: 15.7 us -> 1.94 us
    all_gather x3 -> x0, waiting for transfers between devices: 205 us -> none  [local(): lax.all_gather(modal, 'sub', axis=0, tiled=True)]
    pallas_call x0 -> x1, Pallas kernels: none -> 201 us  [local(): pl.pallas_call(kernel, out_shape=(jax.ShapeDtypeStruct((NI, K), F32), jax...]
    psum x3 -> x0, blocking collectives: 186 us -> none  [local(): lax.psum((jnp.sum(share * residual * image, axis=0), jnp.sum(share * imag...]
    dot_general x12 -> x0, matrix products: 117 us -> none  [the longest x3 83.5 us: local(): jnp.dot(schur, direction, precision=highest, preferred_element_type=jnp.f...]
    ppermute x14 -> x0, starting transfers between devices: 81.4 us -> none  [passed_along(): return lax.ppermute(value, axis, pairs)]
    scatter-add x16 -> x0, other arithmetic: 81 us -> none  [the longest x7 37.7 us: assemble(): merged = field.at[left_index].add(from_left, mode='drop')]
    gather x15 -> x0, local copies, waits for them, and re-layouts: 75 us -> none  [the longest x14 47.1 us: take_rows(): return jnp.take(field, indices, axis=0, mode='fill', fill_value=0.0)]
    ppermute x14 -> x0, waiting for transfers between devices: 33.2 us -> none  [passed_along(): return lax.ppermute(value, axis, pairs)]
  transfers between devices with their start and end apart: 17 -> 0, of which waited for: 8 -> 0; matrix products, arithmetic and copies ran while one was open for 10% -> 0% of each run, Pallas kernels for 0% -> 0%
where the time goes in v1:
time: 209 us
  Pallas kernels  201 us (96%)
  local copies, waits for them, and re-layouts  6.52 us (3%)
    pallas_call x1, Pallas kernels, local(): pl.pallas_call(kernel, out_shape=(jax.ShapeDtypeStruct((NI, K), F32), jax...  201 us
    unnamed x7, local copies, waits for them, and re-layouts  4.9 us

profile of v1, /device:TPU:1, one launch (start us, length us, event | category | flops | bytes accessed | tf_op | source)
XLA Modules:
  0.0 209.0 jit_solution(3673801439034493476)
XLA Ops:
  1.9 0.7 constant_dynamic-update-slice_fusion.1
  2.6 0.7 constant_dynamic-update-slice_fusion.index_row
  3.3 0.0 copy-start.1
  3.3 0.9 copy.10.index_column
  4.2 0.0 copy-done.1
  4.2 200.6 %shard_map.95 = (f32[1792,256]{1,0:T(8,128)}, f32[1792,256]{1,0:T(8,128)}) custom-call(f32[1792,256]{1,0:T(8,128)} %load.1, f32[1792,1792]{1,0:T(8,128)} %schur.1, f32[1792,128]{1,0:T(8,128)} %modes.1, f32[128,4096]{1,0:T(8,128)} %coarse.1, s32[1]{0:T(128)S(6)} %copy.14.live_rows, s32[1]{0:T(128)S(6)} %copy.15.mode_count, s32[1,768]{1,0:T(1,128)} %copy-done.1, ...), custom_call_target="tpu_custom_call" | custom-call | flops 20000000000 | bytes 21000000 | tf_op jit(solution)/shard_map/pallas_call | solution.py:486
  204.8 0.0 copy-start
  204.8 3.0 %copy.16 = f32[1792,256]{1,0:T(8,128)} copy(f32[1792,256]{1,0:T(8,128)} %get-tuple-element.4) | data formatting | bytes 3670016
  207.8 0.0 copy-done
  207.8 1.2 copy.17
Async XLA Ops:
  3.3 0.9 copy-start.1
  204.8 3.0 %copy-start = (f32[1792,256]{1,0:T(8,128)S(1)}, f32[1792,256]{1,0:T(8,128)}, u32[]{:S(2)}) copy-start(f32[1792,256]{1,0:T(8,128)} %get-tuple-element.5) | copy-start | bytes 5505028

commit v2 on v1

--- a/solution.py
+++ b/solution.py
@@ -17,10 +17,11 @@
 ITERS = 3
 W = 128
 STREAMS = K // W
-TILE = 256
+TILE = 448
 ROW_TILES = NI // TILE
 CHUNK = 128
 CHUNKS = NI // CHUNK
+BUFFERS = 4
 
 ZY = [(2, 1), (2, 0), (1, 1), (3, 1), (1, 0), (3, 0), (0, 1), (0, 0)]
 YC = [(dy, dc) for dy in (2, 1, 3, 0) for dc in (1, 0) if (dy, dc) != (0, 0)]
@@ -51,11 +52,12 @@
 
 
 def kernel(
-    load, schur, modes, coarse, live_rows, mode_count, index_row, index_column,
+    load, schur, modes, coarse, live_rows, mode_count, left_rows, right_rows,
     x_out, r_out,
-    s_hi, s_lo, ss_hi, ss_lo, chunk, to_slots, from_slots, phi, phit_hi, phit_lo, phi3_hi, phi3_lo,
+    s_hi, s_lo, chunk, to_slots, from_slots, phi, phit_hi, phit_lo, phi3_hi, phi3_lo, b_hi, b_lo,
     c_in, c_hi, c_lo, share, delta, pair_send, pair_recv,
-    w_buf, d_buf, two, e_send, e_recv, ag, ag_two, rs_send, rs_recv, corr, corr_w, corr_two, ar_send, ar_recv,
+    w_buf, scaled_hi, scaled_lo, smooth, smooth_w, two, e_two, e_send, e_recv, ag, ag_two, rs_send, rs_recv,
+    corr, corr_w, corr_sum, corr_two, sum_two, ar_send, ar_recv,
     local_sem, chunk_sem, send_sem, recv_sem,
 ):
     c = lax.axis_index("cluster")
@@ -84,7 +86,6 @@
         return ZY.index(((4 - dz) % 4, (2 - dy) % 2))
 
     counter = [0]
-    started = []
 
     def send(src, dst, peer):
         n = counter[0]
@@ -111,13 +112,13 @@
         copy.start()
 
     def chunk_copy(i):
-        slot = lax.rem(i, 2)
+        slot = lax.rem(i, BUFFERS)
         return pltpu.make_async_copy(
             schur.at[pl.ds(pl.multiple_of(i * CHUNK, CHUNK), CHUNK)], chunk.at[slot], chunk_sem.at[slot]
         )
 
-    chunk_copy(0).start()
-    chunk_copy(1).start()
+    for i in range(BUFFERS):
+        chunk_copy(i).start()
 
     peers = [ring(1), ring(-1)]
     peers += [x_peer(d) for d in THREE]
@@ -129,12 +130,14 @@
 
     live_count = live_rows[0]
     modes_live = mode_count[0]
-
-    def build_slots(rows, base):
-        local = lax.broadcasted_iota(jnp.int32, (TILE, NI), 1)
-        from_slots[rows] = (local == index_column[rows]).astype(F32).astype(BF16)
-
-    each_tile(2 * NS // TILE, TILE, build_slots)
+    sides = (left_rows, right_rows)
+
+    for side in range(2):
+        column = jnp.broadcast_to(sides[side][...].astype(F32), (128, NS)).T
+        lanes = lax.broadcasted_iota(jnp.int32, (NS, 128), 1).astype(F32)
+        for part in range(NI // 128):
+            hot = jnp.where(lanes + float(part * 128) == column, 1.0, 0.0)
+            from_slots[pl.ds(side * NS, NS), pl.ds(part * 128, 128)] = hot.astype(BF16)
 
     def live_mask(base, shape):
         return (lax.broadcasted_iota(jnp.int32, shape, 0) + base) < live_count
@@ -150,15 +153,6 @@
         each_tile(ROW_TILES, TILE, mask_load)
 
     pl.semaphore_wait(barrier, len(peers))
-
-    c_copies = [
-        send(
-            coarse.at[:, pl.ds(pl.multiple_of(zy_line(dz, dy) * 512, 512), 512)],
-            c_in.at[back(dz, dy)],
-            zy_peer(dz, dy),
-        )
-        for dz, dy in ZY[:-1]
-    ]
 
     def exchange(src, dst):
         return [
@@ -174,54 +168,33 @@
         for copy in copies:
             copy.wait_send()
 
-    def zeros8():
-        return jnp.zeros((8, W), F32)
-
-    def fold8(value):
-        return jnp.sum(value.reshape(TILE // 8, 8, W), axis=0)
-
     def stream(h):
+        columns = pl.ds(h * W, W)
         e_copies = []
+        everything = []
 
         def send_shared(t):
+            def gather(rows, base):
+                e_send[h, rows] = halves(dot(from_slots[rows], two[h]))
+
+            each_tile(2, NS, gather)
             e_copies.append(exchange(e_send.at[h], e_recv.at[h, t]))
-
-        def gather_load(rows, base):
-            e_send[h, rows] = halves(dot(from_slots[rows], two[h]))
-
-        each_tile(2 * NS // TILE, TILE, gather_load)
-        send_shared(0)
-        yield
 
         def receive_shared(t):
             arrived(e_copies[t])
 
             def cut(rows, base):
-                e_two_rows = split(e_recv[h, t, rows])
-                e_two[rows] = e_two_rows
-
-            each_tile(2 * NS // TILE, TILE, cut)
-
-        e_two = two.at[STREAMS]
+                e_two[rows] = split(e_recv[h, t, rows])
+
+            each_tile(2, NS, cut)
 
         def scattered(rows):
-            return halves(dot(to_slots[rows], e_two[pl.ds(0, 2 * NS)]))
+            return halves(dot(to_slots[rows], e_two[...]))
 
         def modal_and_gather(t):
             modal = halves(dot(phit_hi[...], two[h]) + dot(phit_lo[...], two[h]))
             ag[h, t, xx] = modal
             return [send(ag.at[h, t, xx], ag.at[h, t, xx], x_peer(d)) for d in THREE]
-
-        receive_shared(0)
-
-        def first_residual(rows, base):
-            value = w_buf[h, rows] + scattered(rows)
-            r_out[rows, pl.ds(h * W, W)] = value
-            two[h, rows] = split(value)
-
-        each_tile(ROW_TILES, TILE, first_residual)
-        ag_copies = modal_and_gather(0)
-        yield
 
         def reduce_x(t):
             return [send(ar_send.at[h, t, 0], ar_recv.at[h, t, i], x_peer(d)) for i, d in enumerate(THREE)]
@@ -245,9 +218,21 @@
             denominator = jnp.sum(total[8:], axis=0, keepdims=True)
             return numerator / (denominator + 1e-06)
 
+        send_shared(0)
+        yield
+        receive_shared(0)
+
+        def first_residual(rows, base):
+            value = w_buf[h, rows] + scattered(rows)
+            r_out[rows, columns] = value
+            two[h, rows] = split(value)
+
+        each_tile(ROW_TILES, TILE, first_residual)
+        ag_copies = modal_and_gather(0)
+        yield
+
         rs_copies = []
         ar_x = ar_z = ar_y = None
-        everything = []
         for t in range(ITERS):
             arrived(ag_copies)
             everything += ag_copies
@@ -288,38 +273,29 @@
             for i in range(3):
                 value = corr_w[h, t, i]
                 if t > 0:
+                    step = alpha * corr[h, i]
+                    corr_sum[h, i] = step if t == 1 else corr_sum[h, i] + step
                     value = corr[h, i] - alpha * value
                 corr[h, i] = value
                 corr_two[h, pl.ds(i * NM, NM)] = split(value)
 
-            def make_direction(rows, base):
-                columns = pl.ds(h * W, W)
-                coarse_part = halves(dot(phi3_hi[rows], corr_two[h]) + dot(phi3_lo[rows], corr_two[h]))
-                residual = r_out[rows, columns]
+            def make_product(rows, base):
+                value = smooth[rows, columns]
                 if t > 0:
-                    residual = residual - alpha * w_buf[h, rows]
-                    r_out[rows, columns] = residual
-                    step = alpha * d_buf[h, rows]
+                    value = value - alpha * smooth_w[rows, columns]
+                    smooth[rows, columns] = value
+                    residual = r_out[rows, columns]
+                    step = alpha * residual
                     x_out[rows, columns] = step if t == 1 else x_out[rows, columns] + step
-                value = delta[rows] * residual + coarse_part
-                d_buf[h, rows] = value
+                    r_out[rows, columns] = residual - alpha * w_buf[h, rows]
+                value = value + halves(dot(b_hi[rows], corr_two[h]) + dot(b_lo[rows], corr_two[h]))
+                value = jnp.where(live_mask(base, (TILE, W)), value, 0.0)
+                w_buf[h, rows] = value
                 two[h, rows] = split(value)
 
-            each_tile(ROW_TILES, TILE, make_direction)
+            each_tile(ROW_TILES, TILE, make_product)
             left(e_copies[t])
-
-            def shared_product(rows, base):
-                e_send[h, rows] = halves(dot(ss_hi[rows], two[h]) + dot(ss_lo[rows], two[h]))
-
-            each_tile(2 * NS // TILE, TILE, shared_product)
             send_shared(t + 1)
-            yield
-
-            def product(rows, base):
-                value = halves(dot(s_hi[rows], two[h]) + dot(s_lo[rows], two[h]))
-                w_buf[h, rows] = jnp.where(live_mask(base, (TILE, W)), value, 0.0)
-
-            each_tile(ROW_TILES, TILE, product)
             yield
             receive_shared(t + 1)
 
@@ -330,13 +306,18 @@
                 w_buf[h, rows] = value
                 if t < ITERS - 1:
                     two[h, rows] = split(value)
+                    both = split(delta[rows] * value)
+                    scaled_hi[rows, columns] = both[:, :W]
+                    scaled_lo[rows, columns] = both[:, W:]
                 weighted = share[rows] * value
+                fold = lambda v: jnp.sum(v.reshape(TILE // 8, 8, W), axis=0)
                 return (
-                    sums[0] + fold8(weighted * r_out[rows, pl.ds(h * W, W)]),
-                    sums[1] + fold8(weighted * value),
+                    sums[0] + fold(weighted * r_out[rows, columns]),
+                    sums[1] + fold(weighted * value),
                 )
 
-            numerator, denominator = lax.fori_loop(0, ROW_TILES, make_image, (zeros8(), zeros8()))
+            nothing = jnp.zeros((8, W), F32)
+            numerator, denominator = lax.fori_loop(0, ROW_TILES, make_image, (nothing, nothing))
             ar_send[h, t, 0, pl.ds(0, 8)] = numerator
             ar_send[h, t, 0, pl.ds(8, 8)] = denominator
             ar_x = reduce_x(t)
@@ -350,23 +331,36 @@
         alpha = reduced(ITERS - 1, ar_y)
 
         def finish(rows, base):
-            columns = pl.ds(h * W, W)
             r_out[rows, columns] = r_out[rows, columns] - alpha * w_buf[h, rows]
-            x_out[rows, columns] = x_out[rows, columns] + alpha * d_buf[h, rows]
+            x_out[rows, columns] = x_out[rows, columns] + alpha * smooth_w[rows, columns]
 
         each_tile(ROW_TILES, TILE, finish)
         left(everything + ar_x + ar_z + ar_y + rs_copies + e_copies[ITERS])
         yield
 
     streams = [stream(h) for h in range(STREAMS)]
-    for one in streams:
-        next(one)
+
+    def advance():
+        for one in streams:
+            next(one)
+
+    advance()
+    c_copies = [
+        send(
+            coarse.at[:, pl.ds(pl.multiple_of(zy_line(dz, dy) * 512, 512), 512)],
+            c_in.at[back(dz, dy)],
+            zy_peer(dz, dy),
+        )
+        for dz, dy in ZY[:-1]
+    ]
 
     def build_rows(rows, base):
-        local = lax.broadcasted_iota(jnp.int32, (TILE, 2 * NS), 0) + base
-        hot = (local == index_row[...]).astype(F32)
-        to_slots[rows] = hot.astype(BF16)
-        counted = jnp.sum(hot, axis=1, keepdims=True)
+        local = lax.broadcasted_iota(jnp.int32, (TILE, NS), 0) + base
+        counted = jnp.zeros((TILE, 1), F32)
+        for side in range(2):
+            hot = jnp.where(local == sides[side][...], 1.0, 0.0)
+            to_slots[rows, pl.ds(side * NS, NS)] = hot.astype(BF16)
+            counted = counted + jnp.sum(hot, axis=1, keepdims=True)
         alive = jnp.where(live_mask(base, (TILE, 1)), 1.0, 0.0)
         share[rows] = jnp.broadcast_to(alive / (1.0 + counted), (TILE, W))
 
@@ -374,7 +368,7 @@
 
     def cut_chunk(i, carry):
         chunk_copy(i).wait()
-        slot = lax.rem(i, 2)
+        slot = lax.rem(i, BUFFERS)
         base = pl.multiple_of(i * CHUNK, CHUNK)
         rows = pl.ds(base, CHUNK)
         for part in range(7):
@@ -393,46 +387,38 @@
 
     def cut_and_next(i, carry):
         cut_chunk(i, carry)
-        chunk_copy(i + 2).start()
+        chunk_copy(i + BUFFERS).start()
         return carry
 
-    lax.fori_loop(0, CHUNKS - 2, cut_and_next, 0)
-    lax.fori_loop(CHUNKS - 2, CHUNKS, cut_chunk, 0)
+    lax.fori_loop(0, CHUNKS - BUFFERS, cut_and_next, 0)
+    lax.fori_loop(CHUNKS - BUFFERS, CHUNKS, cut_chunk, 0)
 
     loads[STREAMS].wait()
-    mode_mask = lax.broadcasted_iota(jnp.int32, (TILE, NM), 1) < modes_live
+    mode_mask = lax.broadcasted_iota(jnp.int32, (256, NM), 1) < modes_live
 
     def weigh_modes(rows, base):
         value = jnp.where(mode_mask, share[rows] * phi[rows], 0.0)
         both = split(value)
         phi3_hi[rows, pl.ds(0, NM)] = both[:, :NM]
         phi3_lo[rows, pl.ds(0, NM)] = both[:, NM:]
-        phit_hi[:, rows] = value.T.astype(BF16)
-        phit_lo[:, rows] = both[:, NM:].astype(F32).T.astype(BF16)
-        two[STREAMS, rows] = split(delta[rows])
-
-    each_tile(ROW_TILES, TILE, weigh_modes)
+        turned = value.T
+        high = turned.astype(BF16)
+        phit_hi[:, rows] = high
+        phit_lo[:, rows] = (turned - high.astype(F32)).astype(BF16)
+        scale = split(delta[rows])
+        scaled_hi[rows] = jnp.concatenate([both[:, :NM], scale[:, :NM]], axis=1)
+        scaled_lo[rows] = jnp.concatenate([both[:, NM:], scale[:, NM:]], axis=1)
+
+    each_tile(7, 256, weigh_modes)
 
     def gather_pair(rows, base):
         hot = from_slots[rows]
-        pair_send[rows, pl.ds(0, NM)] = dot(hot, phi3_hi[:, pl.ds(0, NM)]) + dot(hot, phi3_lo[:, pl.ds(0, NM)])
-        pair_send[rows, pl.ds(NM, NM)] = halves(dot(hot, two[STREAMS]))
-
-    each_tile(2 * NS // TILE, TILE, gather_pair)
+        pair_send[rows] = dot(hot, scaled_hi[...]) + dot(hot, scaled_lo[...])
+
+    each_tile(2, NS, gather_pair)
     pair_copies = exchange(pair_send, pair_recv)
 
-    for one in streams:
-        next(one)
-
-    def gather_schur(rows, base):
-        hot = from_slots[rows]
-        for part in range(7):
-            columns = pl.ds(part * 256, 256)
-            ss_hi[rows, columns] = dot(hot, s_hi[:, columns]).astype(BF16)
-            ss_lo[rows, columns] = dot(hot, s_lo[:, columns]).astype(BF16)
-
-    each_tile(2 * NS // TILE, TILE, gather_schur)
-
+    advance()
     loads[STREAMS + 1].wait()
     arrived(c_copies)
     for k in range(8):
@@ -440,26 +426,22 @@
         c_hi[pl.ds(k * NM, NM)] = both[:, :512]
         c_lo[pl.ds(k * NM, NM)] = both[:, 512:]
 
-    for one in streams:
-        next(one)
-
     arrived(pair_copies)
 
     def cut_pair(rows, base):
         value = pair_recv[rows]
         high = value.astype(BF16)
-        two[STREAMS, rows] = high
-        pair_send_low[rows] = (value - high.astype(F32)).astype(BF16)
-
-    pair_send_low = two.at[STREAMS + 1]
-    each_tile(2 * NS // TILE, TILE, cut_pair)
+        scaled_hi[rows] = high
+        scaled_lo[rows] = (value - high.astype(F32)).astype(BF16)
+
+    each_tile(2, NS, cut_pair)
 
     def place_pair(rows, base):
         for side in range(2):
             slots = pl.ds(side * NS, NS)
             hot = to_slots[rows, slots]
-            high = dot(hot, two[STREAMS, slots])
-            low = dot(hot, pair_send_low[slots])
+            high = dot(hot, scaled_hi[slots])
+            low = dot(hot, scaled_lo[slots])
             columns = pl.ds((1 + side) * NM, NM)
             phi3_hi[rows, columns] = high[:, :NM].astype(BF16)
             phi3_lo[rows, columns] = low[:, :NM].astype(BF16)
@@ -467,18 +449,74 @@
 
     each_tile(ROW_TILES, TILE, place_pair)
 
-    running = True
-    while running:
-        for one in streams:
-            if next(one, None) is None and one.gi_frame is None:
-                running = False
+    def scale_residual(rows, base):
+        for h in range(STREAMS):
+            columns = pl.ds(h * W, W)
+            both = split(delta[rows] * r_out[rows, columns])
+            scaled_hi[rows, columns] = both[:, :W]
+            scaled_lo[rows, columns] = both[:, W:]
+
+    each_tile(ROW_TILES, TILE, scale_residual)
+
+    def smoother(target, first, last):
+        def tile(i, carry):
+            rows = pl.ds(pl.multiple_of(i * TILE, TILE), TILE)
+            target[rows] = (
+                dot(s_hi[rows], scaled_hi[...]) + dot(s_hi[rows], scaled_lo[...]) + dot(s_lo[rows], scaled_hi[...])
+            )
+            return carry
+
+        lax.fori_loop(first, last, tile, 0)
+
+    def schur_modes(first, last):
+        def tile(i, carry):
+            rows = pl.ds(pl.multiple_of(i * TILE, TILE), TILE)
+            value = dot(s_hi[rows], phi3_hi[...]) + dot(s_hi[rows], phi3_lo[...]) + dot(s_lo[rows], phi3_hi[...])
+            high = value.astype(BF16)
+            b_hi[rows] = high
+            b_lo[rows] = (value - high.astype(F32)).astype(BF16)
+            return carry
+
+        lax.fori_loop(first, last, tile, 0)
+
+    smoother(smooth, 0, 2)
+    advance()
+    smoother(smooth, 2, 4)
+    schur_modes(0, 2)
+    advance()
+    schur_modes(2, 4)
+    advance()
+    for t in range(1, ITERS):
+        advance()
+        smoother(smooth_w, 0, 1)
+        advance()
+        smoother(smooth_w, 1, 3)
+        advance()
+        smoother(smooth_w, 3, 4)
+        advance()
+
+    for h in range(STREAMS):
+        columns = pl.ds(h * W, W)
+        for i in range(3):
+            sum_two[pl.ds(i * NM, NM)] = split(corr_sum[h, i])
+
+        def prolong(rows, base):
+            high, low = phi3_hi[rows], phi3_lo[rows]
+            x_out[rows, columns] = delta[rows] * x_out[rows, columns] + halves(
+                dot(high, sum_two[...]) + dot(low, sum_two[...])
+            )
+            smooth_w[rows, columns] = delta[rows] * r_out[rows, columns] + halves(
+                dot(high, corr_two[h]) + dot(low, corr_two[h])
+            )
+
+        each_tile(ROW_TILES, TILE, prolong)
+    for _ in range(4):
+        advance()
     left(c_copies)
     left(pair_copies)
 
 
 def local(load, schur, modes, coarse_inverse, interface_rows, mode_count, left_rows, right_rows):
-    index_row = jnp.concatenate([left_rows, right_rows], axis=1)
-    index_column = index_row.reshape(2 * NS, 1)
     vmem = pl.BlockSpec(memory_space=pltpu.VMEM)
     smem = pl.BlockSpec(memory_space=pltpu.SMEM)
     anywhere = pl.BlockSpec(memory_space=pl.ANY)
@@ -491,14 +529,14 @@
         scratch_shapes=[
             pltpu.VMEM((NI, NI), BF16),
             pltpu.VMEM((NI, NI), BF16),
-            pltpu.VMEM((2 * NS, NI), BF16),
-            pltpu.VMEM((2 * NS, NI), BF16),
-            pltpu.VMEM((2, CHUNK, NI), F32),
+            pltpu.VMEM((BUFFERS, CHUNK, NI), F32),
             pltpu.VMEM((NI, 2 * NS), BF16),
             pltpu.VMEM((2 * NS, NI), BF16),
             pltpu.VMEM((NI, NM), F32),
             pltpu.VMEM((NM, NI), BF16),
             pltpu.VMEM((NM, NI), BF16),
+            pltpu.VMEM((NI, 3 * NM), BF16),
+            pltpu.VMEM((NI, 3 * NM), BF16),
             pltpu.VMEM((NI, 3 * NM), BF16),
             pltpu.VMEM((NI, 3 * NM), BF16),
             pltpu.VMEM((8, NM, 512), F32),
@@ -509,8 +547,12 @@
             pltpu.VMEM((2 * NS, 2 * NM), F32),
             pltpu.VMEM((2 * NS, 2 * NM), F32),
             pltpu.VMEM((STREAMS, NI, W), F32),
-            pltpu.VMEM((STREAMS, NI, W), F32),
-            pltpu.VMEM((STREAMS + 2, NI, 2 * W), BF16),
+            pltpu.VMEM((NI, K), BF16),
+            pltpu.VMEM((NI, K), BF16),
+            pltpu.VMEM((NI, K), F32),
+            pltpu.VMEM((NI, K), F32),
+            pltpu.VMEM((STREAMS, NI, 2 * W), BF16),
+            pltpu.VMEM((2 * NS, 2 * W), BF16),
             pltpu.VMEM((STREAMS, 2 * NS, W), F32),
             pltpu.VMEM((STREAMS, ITERS + 1, 2 * NS, W), F32),
             pltpu.VMEM((STREAMS, ITERS, 4, NM, W), F32),
@@ -519,11 +561,13 @@
             pltpu.VMEM((STREAMS, ITERS, 7, NM, W), F32),
             pltpu.VMEM((STREAMS, 3, NM, W), F32),
             pltpu.VMEM((STREAMS, ITERS, 3, NM, W), F32),
+            pltpu.VMEM((STREAMS, 3, NM, W), F32),
             pltpu.VMEM((STREAMS, 3 * NM, 2 * W), BF16),
+            pltpu.VMEM((3 * NM, 2 * W), BF16),
             pltpu.VMEM((STREAMS, ITERS, 3, 16, W), F32),
             pltpu.VMEM((STREAMS, ITERS, 13, 16, W), F32),
             pltpu.SemaphoreType.DMA((STREAMS + 2,)),
-            pltpu.SemaphoreType.DMA((2,)),
+            pltpu.SemaphoreType.DMA((BUFFERS,)),
             pltpu.SemaphoreType.DMA((copies,)),
             pltpu.SemaphoreType.DMA((copies,)),
         ],
@@ -531,7 +575,7 @@
             collective_id=0, has_side_effects=True, vmem_limit_bytes=62 * 1024 * 1024
         ),
         cost_estimate=pl.CostEstimate(flops=20 * 10**9, bytes_accessed=21 * 10**6, transcendentals=0),
-    )(load, schur, modes, coarse_inverse, interface_rows, mode_count, index_row, index_column)
+    )(load, schur, modes, coarse_inverse, interface_rows, mode_count, left_rows, right_rows)
 
 
 def solution(mesh):

time: 209 us -> 193 us (0.923)
  Pallas kernels: 201 us -> 187 us
  local copies, waits for them, and re-layouts: 6.52 us -> 4.21 us
    pallas_call x1, Pallas kernels: 201 us -> 187 us  [local(): pl.pallas_call(kernel, out_shape=(jax.ShapeDtypeStruct((NI, K), F32), jax...]
    unnamed x7 -> x4, local copies, waits for them, and re-layouts: 4.9 us -> 4.21 us
where the time goes in v2:
time: 193 us
  Pallas kernels  187 us (97%)
  local copies, waits for them, and re-layouts  4.21 us (2%)
  between operations  1.94 us (1%)
    pallas_call x1, Pallas kernels, local(): pl.pallas_call(kernel, out_shape=(jax.ShapeDtypeStruct((NI, K), F32), jax...  187 us
    unnamed x4, local copies, waits for them, and re-layouts  4.21 us

profile of v2, /device:TPU:1, one launch (start us, length us, event | category | flops | bytes accessed | tf_op | source)
XLA Modules:
  0.0 192.7 jit_solution(8266039850190395036)
XLA Ops:
  1.9 186.5 %shard_map.95 = (f32[1792,256]{1,0:T(8,128)}, f32[1792,256]{1,0:T(8,128)}) custom-call(f32[1792,256]{1,0:T(8,128)} %load.1, f32[1792,1792]{1,0:T(8,128)} %schur.1, f32[1792,128]{1,0:T(8,128)} %modes.1, f32[128,4096]{1,0:T(8,128)} %coarse.1, s32[1]{0:T(128)S(6)} %copy.12.live_rows, s32[1]{0:T(128)S(6)} %copy.13.mode_count, s32[1,384]{1,0:T(1,128)} %left_rows.1, ...), custom_call_target="tpu_custom_call" | custom-call | flops 20000000000 | bytes 21000000 | tf_op jit(solution)/shard_map/pallas_call | solution.py:524
  188.5 0.0 copy-start
  188.5 3.0 %copy.14 = f32[1792,256]{1,0:T(8,128)} copy(f32[1792,256]{1,0:T(8,128)} %get-tuple-element.4) | data formatting | bytes 3670016
  191.5 0.0 copy-done
  191.5 1.2 copy.15
Async XLA Ops:
  188.5 3.0 %copy-start = (f32[1792,256]{1,0:T(8,128)S(1)}, f32[1792,256]{1,0:T(8,128)}, u32[]{:S(2)}) copy-start(f32[1792,256]{1,0:T(8,128)} %get-tuple-element.5) | copy-start | bytes 5505028

commit v3 on v2

--- a/solution.py
+++ b/solution.py
@@ -54,7 +54,7 @@
 def kernel(
     load, schur, modes, coarse, live_rows, mode_count, left_rows, right_rows,
     x_out, r_out,
-    s_hi, s_lo, chunk, to_slots, from_slots, phi, phit_hi, phit_lo, phi3_hi, phi3_lo, b_hi, b_lo,
+    s_hi, s_lo, chunk, to_slots, from_slots, phi, phit_hi, phit_lo, phi3, b_hi, b_lo,
     c_in, c_hi, c_lo, share, delta, pair_send, pair_recv,
     w_buf, scaled_hi, scaled_lo, smooth, smooth_w, two, e_two, e_send, e_recv, ag, ag_two, rs_send, rs_recv,
     corr, corr_w, corr_sum, corr_two, sum_two, ar_send, ar_recv,
@@ -85,6 +85,8 @@
     def back(dz, dy):
         return ZY.index(((4 - dz) % 4, (2 - dy) % 2))
 
+    phi3_hi = phi3.at[:, pl.ds(0, 3 * NM)]
+    phi3_lo = phi3.at[:, pl.ds(3 * NM, 3 * NM)]
     counter = [0]
 
     def send(src, dst, peer):
@@ -338,13 +340,6 @@
         left(everything + ar_x + ar_z + ar_y + rs_copies + e_copies[ITERS])
         yield
 
-    streams = [stream(h) for h in range(STREAMS)]
-
-    def advance():
-        for one in streams:
-            next(one)
-
-    advance()
     c_copies = [
         send(
             coarse.at[:, pl.ds(pl.multiple_of(zy_line(dz, dy) * 512, 512), 512)],
@@ -354,6 +349,13 @@
         for dz, dy in ZY[:-1]
     ]
 
+    streams = [stream(h) for h in range(STREAMS)]
+
+    def advance():
+        for one in streams:
+            next(one)
+
+    advance()
     def build_rows(rows, base):
         local = lax.broadcasted_iota(jnp.int32, (TILE, NS), 0) + base
         counted = jnp.zeros((TILE, 1), F32)
@@ -419,12 +421,6 @@
     pair_copies = exchange(pair_send, pair_recv)
 
     advance()
-    loads[STREAMS + 1].wait()
-    arrived(c_copies)
-    for k in range(8):
-        both = split(c_in[k])
-        c_hi[pl.ds(k * NM, NM)] = both[:, :512]
-        c_lo[pl.ds(k * NM, NM)] = both[:, 512:]
 
     arrived(pair_copies)
 
@@ -471,7 +467,7 @@
     def schur_modes(first, last):
         def tile(i, carry):
             rows = pl.ds(pl.multiple_of(i * TILE, TILE), TILE)
-            value = dot(s_hi[rows], phi3_hi[...]) + dot(s_hi[rows], phi3_lo[...]) + dot(s_lo[rows], phi3_hi[...])
+            value = halves(dot(s_hi[rows], phi3[...])) + dot(s_lo[rows], phi3_hi[...])
             high = value.astype(BF16)
             b_hi[rows] = high
             b_lo[rows] = (value - high.astype(F32)).astype(BF16)
@@ -480,6 +476,12 @@
         lax.fori_loop(first, last, tile, 0)
 
     smoother(smooth, 0, 2)
+    loads[STREAMS + 1].wait()
+    arrived(c_copies)
+    for k in range(8):
+        both = split(c_in[k])
+        c_hi[pl.ds(k * NM, NM)] = both[:, :512]
+        c_lo[pl.ds(k * NM, NM)] = both[:, 512:]
     advance()
     smoother(smooth, 2, 4)
     schur_modes(0, 2)
@@ -535,8 +537,7 @@
             pltpu.VMEM((NI, NM), F32),
             pltpu.VMEM((NM, NI), BF16),
             pltpu.VMEM((NM, NI), BF16),
-            pltpu.VMEM((NI, 3 * NM), BF16),
-            pltpu.VMEM((NI, 3 * NM), BF16),
+            pltpu.VMEM((NI, 6 * NM), BF16),
             pltpu.VMEM((NI, 3 * NM), BF16),
             pltpu.VMEM((NI, 3 * NM), BF16),
             pltpu.VMEM((8, NM, 512), F32),

time: 193 us -> 187 us (0.969)
  Pallas kernels: 187 us -> 180 us
    pallas_call x1, Pallas kernels: 187 us -> 180 us  [local(): pl.pallas_call(kernel, out_shape=(jax.ShapeDtypeStruct((NI, K), F32), jax...]
where the time goes in v3:
time: 187 us
  Pallas kernels  180 us (96%)
  local copies, waits for them, and re-layouts  4.21 us (2%)
  between operations  1.94 us (1%)
    pallas_call x1, Pallas kernels, local(): pl.pallas_call(kernel, out_shape=(jax.ShapeDtypeStruct((NI, K), F32), jax...  180 us
    unnamed x4, local copies, waits for them, and re-layouts  4.21 us

profile of v3, /device:TPU:1, one launch (start us, length us, event | category | flops | bytes accessed | tf_op | source)
XLA Modules:
  0.0 186.5 jit_solution(13938647192651226490)
XLA Ops:
  1.9 180.4 %shard_map.95 = (f32[1792,256]{1,0:T(8,128)}, f32[1792,256]{1,0:T(8,128)}) custom-call(f32[1792,256]{1,0:T(8,128)} %load.1, f32[1792,1792]{1,0:T(8,128)} %schur.1, f32[1792,128]{1,0:T(8,128)} %modes.1, f32[128,4096]{1,0:T(8,128)} %coarse.1, s32[1]{0:T(128)S(6)} %copy.12.live_rows, s32[1]{0:T(128)S(6)} %copy.13.mode_count, s32[1,384]{1,0:T(1,128)} %left_rows.1, ...), custom_call_target="tpu_custom_call" | custom-call | flops 20000000000 | bytes 21000000 | tf_op jit(solution)/shard_map/pallas_call | solution.py:526
  182.3 0.0 copy-start
  182.3 3.0 %copy.14 = f32[1792,256]{1,0:T(8,128)} copy(f32[1792,256]{1,0:T(8,128)} %get-tuple-element.4) | data formatting | bytes 3670016
  185.3 0.0 copy-done
  185.3 1.2 copy.15
Async XLA Ops:
  182.3 3.0 %copy-start = (f32[1792,256]{1,0:T(8,128)S(1)}, f32[1792,256]{1,0:T(8,128)}, u32[]{:S(2)}) copy-start(f32[1792,256]{1,0:T(8,128)} %get-tuple-element.5) | copy-start | bytes 5505028
